TPU v7x, 32 devices: a whole 2x2x4 slice. The times are simulated.
32 devices in a mesh: dp: 8 (over z, core), expert: 4 (over y, x).
Axes of the slice: x: 2, y: 2, z: 4, core: 2. Of those that a mesh axis runs over, the one named last changes fastest.
Arguments:
- route_ids: int32 [4096, 2], P(('dp', 'expert')), may hold values from 0 to 3, all different within a row; in each aligned block of 128 rows (0 to 127, 128 to 255, ...) at most 80 rows name the same one
- gate_values: float32 [4096, 2], P(('dp', 'expert')), may hold values from 0.1 to 1
- out_grad: bfloat16 [4096, 2048], P(('dp', 'expert')), may hold values from -4 to 4
- down_weight: bfloat16 [4, 768, 2048], P('expert'), may hold values from -0.21875 to 0.21875
- hidden: bfloat16 [8, 4, 4, 80, 768], P('dp', 'expert'), may hold values from -6 to 6
Outputs:
- mixed_out: bfloat16 [4096, 2048], P(('dp', 'expert'))
- gate_grad: float32 [4096, 2], P(('dp', 'expert'))
- hidden_grad: bfloat16 [8, 4, 4, 80, 768], P('dp', 'expert')
- weight_grad: float32 [4, 768, 2048], P('expert', 'dp')
Inputs may be any that keep to these rules, and one draw needn't show every extreme that they name: `route_ids`: each row names 2 different experts. Among the rows of one device no expert is named by more than 80 rows, and in every draw some device names some expert exactly 80 times.
All inputs are finite; a program needn't handle non-finite values.
Results may differ from a plain program's by a relative error of at most 0.0049.
Values may be sent and summed in bfloat16 or wider, within the bound.
A program may use at most 64 MiB of HBM per device.

v0:
```python
import jax
import jax.numpy as jnp
from jax import lax
from jax.sharding import PartitionSpec as P


def slot_table(route_ids, experts, capacity):
    flat_ids = route_ids.reshape(-1)
    route_count = flat_ids.shape[0]
    onehot = (flat_ids[:, None] == jnp.arange(experts, dtype=jnp.int32)[None, :]).astype(
        jnp.float32
    )
    positions = jnp.arange(route_count, dtype=jnp.int32)
    earlier = (positions[:, None] > positions[None, :]).astype(jnp.float32)
    before = jnp.dot(
        earlier, onehot, precision=lax.Precision.HIGHEST, preferred_element_type=jnp.float32
    )
    slot_rank = jnp.sum(before * onehot, axis=1).astype(jnp.int32)
    slot_index = flat_ids * capacity + slot_rank
    slots_all = jnp.arange(experts * capacity, dtype=jnp.int32)
    return (slots_all[:, None] == slot_index[None, :]).astype(jnp.bfloat16)


def on_device(route_ids, gate_values, out_grad, down_weight, hidden):
    experts = lax.axis_size("expert")
    capacity = hidden.shape[3]
    inner_width = hidden.shape[4]
    feature_width = out_grad.shape[1]
    tok_rows = route_ids.shape[0]
    routes = route_ids.shape[1]
    slot_map = slot_table(route_ids, experts, capacity)
    weight_mat = down_weight[0]
    rows_in = hidden.reshape(-1, inner_width)
    expert_out = jnp.dot(rows_in, weight_mat, preferred_element_type=jnp.float32)
    expert_out = expert_out.astype(jnp.bfloat16).reshape(experts, capacity, feature_width)
    grads_f = out_grad.astype(jnp.float32)
    scaled = (
        (gate_values[:, :, None] * grads_f[:, None, :])
        .reshape(-1, feature_width)
        .astype(jnp.bfloat16)
    )
    outgoing = jnp.dot(slot_map, scaled, preferred_element_type=jnp.float32)
    outgoing = outgoing.astype(jnp.bfloat16).reshape(experts, capacity, feature_width)
    returned = lax.all_to_all(expert_out, "expert", split_axis=0, concat_axis=0, tiled=True)
    incoming = lax.all_to_all(outgoing, "expert", split_axis=0, concat_axis=0, tiled=True)
    gathered = jnp.einsum(
        "sr,sd->rd",
        slot_map,
        returned.reshape(-1, feature_width),
        preferred_element_type=jnp.float32,
    )
    gathered = gathered.reshape(tok_rows, routes, feature_width)
    mixed_out = jnp.sum(gate_values[:, :, None] * gathered, axis=1).astype(jnp.bfloat16)
    gate_grad = jnp.sum(gathered * grads_f[:, None, :], axis=2)
    grad_rows = incoming.reshape(-1, feature_width)
    hidden_grad = jnp.einsum("sd,hd->sh", grad_rows, weight_mat, preferred_element_type=jnp.float32)
    hidden_grad = hidden_grad.astype(jnp.bfloat16).reshape(hidden.shape)
    partial_term = jnp.einsum("sh,sd->hd", rows_in, grad_rows, preferred_element_type=jnp.float32)
    weight_grad = lax.psum_scatter(partial_term, "dp", scatter_dimension=0, tiled=True)
    return (mixed_out, gate_grad, hidden_grad, weight_grad[None])


def solution(mesh):
    in_specs = (
        P(("dp", "expert"), None),
        P(("dp", "expert"), None),
        P(("dp", "expert"), None),
        P("expert", None, None),
        P("dp", "expert", None, None, None),
    )
    out_specs = (
        P(("dp", "expert"), None),
        P(("dp", "expert"), None),
        P("dp", "expert", None, None, None),
        P("expert", "dp", None),
    )
    return jax.shard_map(
        on_device, mesh=mesh, in_specs=in_specs, out_specs=out_specs, check_vma=False
    )
```

profile of v0, /device:TPU:0, one launch (start us, length us, event | category | flops | bytes accessed | tf_op | source)
XLA Modules:
  0.0 134.5 jit_solution(8750412218495142814)
XLA Ops:
  7.2 0.0 copy-start
  7.2 0.0 reduce-scatter.4.cloned.1.call-start
  7.2 0.9 copy.15
  8.2 0.1 reshape.70
  8.3 0.2 fusion.10
  8.5 0.8 copy.17
  9.3 0.1 mul.52
  9.4 3.5 %mul.50.clone = f32[128,2,2048]{2,1,0:T(2,128)} broadcast(bf16[128,2048]{1,0:T(8,128)(2,1)} %param.7), dimensions={0,2} | broadcast | bytes 2621440 | tf_op jit(solution)/shard_map/mul | solution.py:54
  12.9 3.7 %mul.54 = f32[256,2048]{1,0:T(8,128)} reshape(f32[128,2,2048]{2,1,0:T(2,128)} %mul.50.clone) | data formatting | bytes 4194304 | tf_op jit(solution)/shard_map/mul | solution.py:54
  16.6 2.2 %convolution_convert_fusion = bf16[320,2048]{1,0:T(8,128)(2,1)S(1)} fusion(f32[256,2048]{1,0:T(8,128)} %mul.54, f32[256]{0:T(256)S(1)} %mul.52, s32[256]{0:T(256)S(1)} %convert_add_fusion), kind=kOutput, calls=%fused_computation.6 | convolution fusion | flops 337330176 | bytes 3409920 | tf_op jit(solution)/shard_map/dot_general | solution.py:42
  18.7 0.0 copy-start.3
  18.8 22.0 %all_to_all.10 = bf16[4,80,2048]{2,1,0:T(8,128)(2,1)S(1)} all-to-all(bf16[4,80,2048]{2,1,0:T(8,128)(2,1)S(1)} %bitcast.28), channel_id=1, replica_groups=mesh['dp'=8,'expert'=4] {'expert'}, dimensions={0} | all-to-all | bytes 2621440 | tf_op jit(solution)/shard_map/all_to_all | solution.py:45
  40.8 0.0 copy-start.1
  40.8 1.1 copy-done.1
  41.9 0.0 copy-done.3
  41.9 4.5 %convolution_bitcast_fusion = f32[768,2048]{0,1:T(8,128)} fusion(bf16[320,2048]{1,0:T(8,128)(2,1)S(1)} %bitcast.26, bf16[320,768]{1,0:T(8,128)(2,1)S(1)} %bitcast.32), kind=kOutput, calls=%fused_computation | convolution fusion | flops 1006632960 | bytes 8093696 | tf_op jit(solution)/shard_map/sh,sd->hd/dot_general | solution.py:58
  46.4 6.6 %copy.20 = f32[768,2048]{1,0:T(8,128)} copy(f32[768,2048]{0,1:T(8,128)} %convolution_bitcast_fusion) | data formatting | bytes 12582912
  53.0 0.0 reduce-scatter.4.cloned.1.call-update
  53.1 0.0 copy-done
  53.1 3.4 %fusion.4 = bf16[320,2048]{1,0:T(8,128)(2,1)} fusion(bf16[320,768]{1,0:T(8,128)(2,1)} %bitcast.31, bf16[1,768,2048]{2,1,0:T(8,128)(2,1)S(1)} %copy-done), kind=kOutput, calls=%fused_computation.5 | convolution fusion | flops 1007288320 | bytes 4947968 | tf_op jit(solution)/shard_map/dot_general | solution.py:34
  56.4 0.0 copy-start.4
  56.4 4.5 %all-to-all-start = ((bf16[4,80,2048]{2,1,0:T(8,128)(2,1)}), bf16[4,80,2048]{2,1,0:T(8,128)(2,1)}, u32[]{:S(2)}, u32[]{:S(2)}) async-start(bf16[4,80,2048]{2,1,0:T(8,128)(2,1)} %bitcast.30), calls=%async_computation | async-start | bytes 2621440 | tf_op jit(solution)/shard_map/all_to_all | solution.py:44
  60.9 2.2 %convert_element_type.31 = f32[128,2048]{1,0:T(8,128)} convert(bf16[128,2048]{1,0:T(8,128)(2,1)} %param.7) | non-fusion elementwise | flops 262144 | bytes 1572864 | tf_op jit(solution)/shard_map/convert_element_type | solution.py:36
  63.1 0.1 iota_compare_fusion
  63.3 0.1 eq.47
  63.4 12.7 %all-to-all-done = bf16[4,80,2048]{2,1,0:T(8,128)(2,1)} async-done(((bf16[4,80,2048]{2,1,0:T(8,128)(2,1)}), bf16[4,80,2048]{2,1,0:T(8,128)(2,1)}, u32[]{:S(2)}, u32[]{:S(2)}) %all-to-all-start) | async-done | bytes 1310752 | tf_op jit(solution)/shard_map/all_to_all | solution.py:44
  76.1 0.0 copy-start.2
  76.1 0.0 copy-done.4
  76.1 3.5 %multiply_reduce_fusion = (f32[128,2]{0,1:T(2,128)}, bf16[128,2048]{1,0:T(8,128)(2,1)}) fusion(f32[128,2048]{1,0:T(8,128)} %convert_element_type.31, f32[128,2]{0,1:T(2,128)S(1)} %copy-done.4, bf16[320,2048,1]{1,0,2:T(8,128)(2,1)} %bitcast.4, pred[128,2,320]{2,1,0:T(4,128)(4,1)S(1)} %eq.47), kind=kOutput, calls=%fused_computation.8 | convolution fusion | flops 337379072 | bytes 2967552 | tf_op jit(solution)/shard_map/sr,sd->rd/dot_general | solution.py:46
  79.7 0.0 copy-done.2
  79.7 2.0 %fusion.7 = bf16[320,768]{1,0:T(8,128)(2,1)} fusion(bf16[320,2048]{1,0:T(8,128)(2,1)S(1)} %bitcast.27, bf16[1,768,2048]{2,1,0:T(8,128)(2,1)S(1)} %copy-done), kind=kOutput, calls=%fused_computation.10 | convolution fusion | flops 1006878720 | bytes 4947968 | tf_op jit(solution)/shard_map/sd,hd->sh/dot_general | solution.py:56
  81.7 41.1 %reduce-scatter.4.cloned.1.call-done = f32[96,2048]{1,0:T(8,128)} async-done(((f32[768,2048]{1,0:T(8,128)}), f32[96,2048]{1,0:T(8,128)}) %reduce-scatter.4.cloned.1.call-update) | async-done | bytes 786448
  122.7 2.5 %copy.21 = f32[96,2048]{0,1:T(8,128)} copy(f32[96,2048]{1,0:T(8,128)} %reduce-scatter.4.cloned.1.call-done) | data formatting | bytes 1572864
  125.2 2.4 %copy.19 = f32[1,96,2048]{2,1,0:T(8,128)} copy(f32[1,96,2048]{1,2,0:T(8,128)} %bitcast.29) | data formatting | bytes 1572864
  (1 shorter events, 0.0 us)
Async XLA Ops:
  7.2 45.9 %copy-start = (bf16[1,768,2048]{2,1,0:T(8,128)(2,1)S(1)}, bf16[1,768,2048]{2,1,0:T(8,128)(2,1)}, u32[]{:S(2)}) copy-start(bf16[1,768,2048]{2,1,0:T(8,128)(2,1)} %param.8) | copy-start | bytes 9437188
  7.2 115.6 %reduce-scatter.4.cloned.1.call-start = ((), (), s32[]{:S(2)}) async-start(), calls=%async_computation.3 | async-start | bytes 7077888
  18.7 23.2 %copy-start.3 = (bf16[1,1,4,80,768]{4,3,2,1,0:T(8,128)(2,1)S(1)}, bf16[1,1,4,80,768]{4,3,2,1,0:T(8,128)(2,1)}, u32[]{:S(2)}) copy-start(bf16[1,1,4,80,768]{4,3,2,1,0:T(8,128)(2,1)} %param.9) | copy-start | bytes 1474564
  40.8 1.1 copy-start.1
  56.4 19.7 %copy-start.4 = (f32[128,2]{0,1:T(2,128)S(1)}, f32[128,2]{0,1:T(2,128)}, u32[]{:S(2)}) copy-start(f32[128,2]{0,1:T(2,128)} %param.6) | copy-start | bytes 3076
  56.4 19.7 %all-to-all-start = ((bf16[4,80,2048]{2,1,0:T(8,128)(2,1)}), bf16[4,80,2048]{2,1,0:T(8,128)(2,1)}, u32[]{:S(2)}, u32[]{:S(2)}) async-start(bf16[4,80,2048]{2,1,0:T(8,128)(2,1)} %bitcast.30), calls=%async_computation | async-start | bytes 2621440 | tf_op jit(solution)/shard_map/all_to_all | solution.py:44
  76.1 3.5 %copy-start.2 = (bf16[4,80,2048]{2,1,0:T(8,128)(2,1)S(1)}, bf16[4,80,2048]{2,1,0:T(8,128)(2,1)}, u32[]{:S(2)}) copy-start(bf16[4,80,2048]{2,1,0:T(8,128)(2,1)} %copy-done.1) | copy-start | bytes 3932164
Sparse Core Ops, SparseCore 0:
  53.2 69.5 reduce-scatter.3
where the time goes:
time: 135 us; the launch traced here: 134 us
  waiting for transfers between devices  53.8 us (40%)
  blocking collectives  22 us (16%)
  local copies, waits for them, and re-layouts  21.9 us (16%)
  matrix products  15.8 us (12%)
  between operations  14.1 us (10%)
  starting transfers between devices  4.53 us (3%)
  other arithmetic  2.31 us (2%)
    unnamed x2, waiting for transfers between devices  41.1 us
    all_to_all x1, blocking collectives, on_device(): lax.all_to_all(outgoing, 'expert', split_axis=0, concat_axis=0, tiled=True)  22 us
    unnamed x15, local copies, waits for them, and re-layouts  14.4 us
    all_to_all x1, waiting for transfers between devices, on_device(): lax.all_to_all(expert_out, 'expert', split_axis=0, concat_axis=0, tiled=T...  12.7 us
    mul x2, local copies, waits for them, and re-layouts, on_device(): gate_grad = jnp.sum(gathered * grads_f[:, None, :], axis=2)  7.11 us
    dot_general x1, matrix products, on_device(): jnp.einsum('sh,sd->hd', rows_in, grad_rows, preferred_element_type=jnp.fl...  4.49 us
    all_to_all x1, starting transfers between devices, on_device(): lax.all_to_all(expert_out, 'expert', split_axis=0, concat_axis=0, tiled=T...  4.49 us
    dot_general x1, matrix products, on_device(): jnp.einsum('sr,sd->rd', slot_map, returned.reshape(-1, feature_width), pr...  3.52 us
  transfers between devices with their start and end apart: 2, of which 2 were waited for; matrix products, arithmetic and copies ran while one was open for 8% of the time, Pallas kernels for 0%

commit v1 on v0

--- a/solution.py
+++ b/solution.py
@@ -1,7 +1,17 @@
+import functools
+
 import jax
 import jax.numpy as jnp
 from jax import lax
+from jax.experimental import pallas as pl
+from jax.experimental.pallas import tpu as pltpu
 from jax.sharding import PartitionSpec as P
+
+
+MESH = pl.DeviceIdType.MESH
+CHUNKS = 8
+F32 = jnp.float32
+BF16 = jnp.bfloat16
 
 
 def slot_table(route_ids, experts, capacity):
@@ -21,7 +31,7 @@
     return (slots_all[:, None] == slot_index[None, :]).astype(jnp.bfloat16)
 
 
-def on_device(route_ids, gate_values, out_grad, down_weight, hidden):
+def on_device_generic(route_ids, gate_values, out_grad, down_weight, hidden):
     experts = lax.axis_size("expert")
     capacity = hidden.shape[3]
     inner_width = hidden.shape[4]
@@ -60,6 +70,302 @@
     return (mixed_out, gate_grad, hidden_grad, weight_grad[None])
 
 
+def fused_kernel(
+    nf, ids_ref, gates_ref, og_ref, w_ref, hid_ref,
+    mixed_ref, gate_ref, hg_ref, wg_ref,
+    hall, ht, sel, sel_t, gslot, gcol, outg, inc, eo, ret, csend, crecv, acc,
+    rsend, rrecv, lsend, lrecv, hgacc, qacc,
+    cot_s, cot_r, eo_s, eo_r, core_s, core_r, rs, rr, ls, lr,
+):
+    dp, me = lax.axis_index("dp"), lax.axis_index("expert")
+    ne = lax.axis_size("expert")
+    nz = lax.axis_size("dp") // 2
+    z, core = lax.div(dp, 2), lax.rem(dp, 2)
+    tok, top = ids_ref.shape
+    cap = inc.shape[2]
+    fc = inc.shape[3]
+    width = hid_ref.shape[1]
+    block = wg_ref.shape[0]
+    slots = ne * cap
+    mate = 2 * z + 1 - core
+
+    barrier = pltpu.get_barrier_semaphore()
+    for d in range(1, ne):
+        pl.semaphore_signal(barrier, inc=1, device_id=(dp, lax.rem(me + d, ne)), device_id_type=MESH)
+    pl.semaphore_signal(barrier, inc=1, device_id=(mate, me), device_id_type=MESH)
+
+    @pl.when(z > 0)
+    def _():
+        pl.semaphore_signal(barrier, inc=1, device_id=(dp - 2, me), device_id_type=MESH)
+
+    @pl.when(z < nz - 1)
+    def _():
+        pl.semaphore_signal(barrier, inc=1, device_id=(dp + 2, me), device_id_type=MESH)
+
+    ids = ids_ref[...]
+    gates = gates_ref[...]
+    row = lax.broadcasted_iota(jnp.int32, (tok, tok), 0)
+    col = lax.broadcasted_iota(jnp.int32, (tok, tok), 1)
+    diagonal = row == col
+    earlier = col < row
+    slot_rows = lax.broadcasted_iota(jnp.int32, (cap, tok), 0).astype(F32)
+    slot_cols = lax.broadcasted_iota(jnp.int32, (tok, cap), 1).astype(F32)
+
+    def to_row(column):
+        return jnp.sum(jnp.where(diagonal, column, 0.0), axis=0, keepdims=True)
+
+    for e in range(ne):
+        named = jnp.sum(jnp.where(ids == e, 1.0, 0.0), axis=1, keepdims=True)
+        gate = jnp.sum(jnp.where(ids == e, gates, 0.0), axis=1, keepdims=True)
+        rank = jnp.sum(jnp.where(earlier, to_row(named), 0.0), axis=1, keepdims=True)
+        place = jnp.where(named > 0.0, rank, -1.0)
+        hit = slot_rows == to_row(place)
+        sel[e] = jnp.where(hit, 1.0, 0.0).astype(BF16)
+        gslot[e] = jnp.sum(jnp.where(hit, to_row(gate), 0.0), axis=1, keepdims=True)
+        sel_t[e] = jnp.where(slot_cols == place, 1.0, 0.0).astype(BF16)
+        gcol[e] = gate
+
+    count = ne + jnp.where(z > 0, 1, 0) + jnp.where(z < nz - 1, 1, 0)
+    pl.semaphore_wait(barrier, count)
+
+    def columns(f):
+        return pl.ds(pl.multiple_of(f * fc, fc), fc)
+
+    def cot_copy(f, d, peer, slot):
+        return pltpu.make_async_remote_copy(
+            src_ref=outg.at[f, d - 1], dst_ref=inc.at[f, slot],
+            send_sem=cot_s.at[f, d - 1], recv_sem=cot_r.at[f, d - 1],
+            device_id=(dp, peer), device_id_type=MESH)
+
+    def eo_copy(f, d, peer, slot):
+        return pltpu.make_async_remote_copy(
+            src_ref=eo.at[f, peer], dst_ref=ret.at[f, slot],
+            send_sem=eo_s.at[f, d - 1], recv_sem=eo_r.at[f, d - 1],
+            device_id=(dp, peer), device_id_type=MESH)
+
+    def core_copy(f):
+        return pltpu.make_async_remote_copy(
+            src_ref=csend.at[f], dst_ref=crecv.at[f],
+            send_sem=core_s.at[f], recv_sem=core_r.at[f],
+            device_id=(mate, me), device_id_type=MESH)
+
+    def up_copy(f, zz):
+        return pltpu.make_async_remote_copy(
+            src_ref=rsend.at[f, zz], dst_ref=rrecv.at[f, zz],
+            send_sem=rs.at[f, zz], recv_sem=rr.at[f, zz],
+            device_id=(lax.rem(dp + 2, 2 * nz), me), device_id_type=MESH)
+
+    def down_copy(f, zz):
+        return pltpu.make_async_remote_copy(
+            src_ref=lsend.at[f, zz], dst_ref=lrecv.at[f, zz],
+            send_sem=ls.at[f, zz], recv_sem=lr.at[f, zz],
+            device_id=(lax.rem(dp + 2 * nz - 2, 2 * nz), me), device_id_type=MESH)
+
+    @pl.loop(0, nf)
+    def _(f):
+        grads = og_ref[:, columns(f)]
+        for d in (*range(1, ne), 0):
+            e = lax.rem(me + d, ne)
+            rows = jnp.dot(sel[e], grads, preferred_element_type=F32)
+            rows = (gslot[e] * rows).astype(BF16)
+            if d:
+                outg[f, d - 1] = rows
+                cot_copy(f, d, e, me).start()
+            else:
+                inc[f, me] = rows
+
+    hall[...] = hid_ref[...].T
+    for zz in range(nz):
+        ht[0, zz] = hall[pl.ds(pl.multiple_of(block * (2 * zz + 1 - core), block), block), :]
+        ht[1, zz] = hall[pl.ds(pl.multiple_of(block * (2 * zz + core), block), block), :]
+    hgacc[...] = jnp.zeros_like(hgacc)
+    qacc[...] = jnp.zeros_like(qacc)
+
+    @pl.loop(0, nf + nz - 1)
+    def _(s):
+        @pl.when(s < nf)
+        def _():
+            f = s
+            weight = w_ref[:, columns(f)]
+            y = jnp.dot(hid_ref[...], weight, preferred_element_type=F32)
+            eo[f] = y.astype(BF16).reshape(ne, cap, fc)
+            for d in range(1, ne):
+                e = lax.rem(me + ne - d, ne)
+                cot_copy(f, d, e, e).wait_recv()
+            x = inc[f].reshape(slots, fc)
+            other = jnp.dot(ht[0].reshape(nz * block, slots), x, preferred_element_type=F32)
+            csend[f] = other.astype(BF16).reshape(nz, block, fc)
+            core_copy(f).start()
+            for d in range(1, ne):
+                e = lax.rem(me + d, ne)
+                eo_copy(f, d, e, me).start()
+            ret[f, me] = eo[f, me]
+            own = jnp.dot(ht[1].reshape(nz * block, slots), x, preferred_element_type=F32)
+            acc[f] = own.reshape(nz, block, fc)
+            hgacc[...] += lax.dot_general(
+                x, weight, (((1,), (1,)), ((), ())), preferred_element_type=F32)
+            core_copy(f).wait_recv()
+            acc[f] += crecv[f].astype(F32)
+
+        up = s - z
+
+        @pl.when((up >= 0) & (up < nf))
+        def _():
+            for zz in range(nz - 1, 0, -1):
+                @pl.when((zz > z) & (z > 0))
+                def _():
+                    up_copy(up, zz).wait_recv()
+                    rsend[up, zz] = (acc[up, zz] + rrecv[up, zz].astype(F32)).astype(BF16)
+                    up_copy(up, zz).start()
+
+                @pl.when((zz > z) & (z == 0))
+                def _():
+                    rsend[up, zz] = acc[up, zz].astype(BF16)
+                    up_copy(up, zz).start()
+
+        down = s - (nz - 1 - z)
+
+        @pl.when((down >= 0) & (down < nf))
+        def _():
+            for zz in range(nz - 1):
+                @pl.when((zz < z) & (z < nz - 1))
+                def _():
+                    down_copy(down, zz).wait_recv()
+                    lsend[down, zz] = (acc[down, zz] + lrecv[down, zz].astype(F32)).astype(BF16)
+                    down_copy(down, zz).start()
+
+                @pl.when((zz < z) & (z == nz - 1))
+                def _():
+                    lsend[down, zz] = acc[down, zz].astype(BF16)
+                    down_copy(down, zz).start()
+
+        back = s - (nz - 1)
+
+        @pl.when(back >= 0)
+        def _():
+            f = back
+            for d in range(1, ne):
+                e = lax.rem(me + ne - d, ne)
+                eo_copy(f, d, e, e).wait_recv()
+            grads = og_ref[:, columns(f)].astype(F32)
+            mixed = jnp.zeros((tok, fc), F32)
+            for e in range(ne):
+                routed = jnp.dot(sel_t[e], ret[f, e], preferred_element_type=F32)
+                mixed += gcol[e] * routed
+                product = routed * grads
+                part = product[:, 0:128]
+                for j in range(128, fc, 128):
+                    part += product[:, j:j + 128]
+                qacc[e] += part
+            mixed_ref[:, columns(f)] = mixed.astype(BF16)
+
+            wg_ref[:, columns(f)] = acc[f, z]
+
+            @pl.when(z > 0)
+            def _():
+                up_copy(f, z).wait_recv()
+                wg_ref[:, columns(f)] += rrecv[f, z].astype(F32)
+
+            @pl.when(z < nz - 1)
+            def _():
+                down_copy(f, z).wait_recv()
+                wg_ref[:, columns(f)] += lrecv[f, z].astype(F32)
+
+    hg_ref[...] = hgacc[...].astype(BF16)
+    parts = []
+    for k in range(top):
+        total = jnp.zeros((tok, 1), F32)
+        for e in range(ne):
+            total += jnp.where(ids[:, k:k + 1] == e, jnp.sum(qacc[e], axis=1, keepdims=True), 0.0)
+        parts.append(total)
+    for k in range(top):
+        gate_ref[:, k:k + 1] = parts[k]
+
+    @pl.loop(0, nf)
+    def _(f):
+        core_copy(f).wait_send()
+        for d in range(1, ne):
+            e = lax.rem(me + d, ne)
+            cot_copy(f, d, e, me).wait_send()
+            eo_copy(f, d, e, me).wait_send()
+        for zz in range(nz):
+            @pl.when(zz > z)
+            def _():
+                up_copy(f, zz).wait_send()
+
+            @pl.when(zz < z)
+            def _():
+                down_copy(f, zz).wait_send()
+
+
+def on_device(route_ids, gate_values, out_grad, down_weight, hidden):
+    ne = lax.axis_size("expert")
+    nz = lax.axis_size("dp") // 2
+    cap, width = hidden.shape[3:]
+    tok, feat = out_grad.shape
+    top = route_ids.shape[1]
+    nf = CHUNKS
+    fc = feat // nf
+    block = width // (2 * nz)
+    slots = ne * cap
+    chain = pltpu.VMEM((nf, nz, block, fc), BF16)
+    dma = pltpu.SemaphoreType.DMA
+    vmem = pl.BlockSpec(memory_space=pltpu.VMEM)
+    mixed, gate, hg, wg = pl.pallas_call(
+        functools.partial(fused_kernel, nf),
+        out_shape=(
+            jax.ShapeDtypeStruct((tok, feat), BF16),
+            jax.ShapeDtypeStruct((tok, top), F32),
+            jax.ShapeDtypeStruct((slots, width), BF16),
+            jax.ShapeDtypeStruct((block, feat), F32),
+        ),
+        in_specs=[vmem] * 5,
+        out_specs=(vmem,) * 4,
+        scratch_shapes=[
+            pltpu.VMEM((width, slots), BF16),
+            pltpu.VMEM((2, nz, block, slots), BF16),
+            pltpu.VMEM((ne, cap, tok), BF16),
+            pltpu.VMEM((ne, tok, cap), BF16),
+            pltpu.VMEM((ne, cap, 1), F32),
+            pltpu.VMEM((ne, tok, 1), F32),
+            pltpu.VMEM((nf, ne - 1, cap, fc), BF16),
+            pltpu.VMEM((nf, ne, cap, fc), BF16),
+            pltpu.VMEM((nf, ne, cap, fc), BF16),
+            pltpu.VMEM((nf, ne, cap, fc), BF16),
+            chain,
+            chain,
+            pltpu.VMEM((nf, nz, block, fc), F32),
+            chain,
+            chain,
+            chain,
+            chain,
+            pltpu.VMEM((slots, width), F32),
+            pltpu.VMEM((ne, tok, 128), F32),
+            dma((nf, ne - 1)),
+            dma((nf, ne - 1)),
+            dma((nf, ne - 1)),
+            dma((nf, ne - 1)),
+            dma((nf,)),
+            dma((nf,)),
+            dma((nf, nz)),
+            dma((nf, nz)),
+            dma((nf, nz)),
+            dma((nf, nz)),
+        ],
+        compiler_params=pltpu.CompilerParams(
+            collective_id=0, has_side_effects=True, vmem_limit_bytes=52 * 1024 * 1024
+        ),
+        cost_estimate=pl.CostEstimate(
+            flops=6 * slots * width * feat, bytes_accessed=2 * width * feat, transcendentals=0
+        ),
+    )(route_ids, gate_values, out_grad, down_weight[0], hidden.reshape(slots, width))
+    return mixed, gate, hg.reshape(hidden.shape), wg[None]
+
+
+def fits(mesh):
+    return mesh.shape["expert"] <= 4 and mesh.shape["dp"] in (2, 4, 8)
+
+
 def solution(mesh):
     in_specs = (
         P(("dp", "expert"), None),
@@ -74,6 +380,7 @@
         P("dp", "expert", None, None, None),
         P("expert", "dp", None),
     )
+    body = on_device if fits(mesh) else on_device_generic
     return jax.shard_map(
-        on_device, mesh=mesh, in_specs=in_specs, out_specs=out_specs, check_vma=False
-    )
+        body, mesh=mesh, in_specs=in_specs, out_specs=out_specs, check_vma=False
+    )

time: 135 us -> 58 us (0.43)
  waiting for transfers between devices: 53.8 us -> 0 us
  Pallas kernels: 0 us -> 50.3 us
  blocking collectives: 22 us -> 0 us
  matrix products: 15.8 us -> 0 us
  local copies, waits for them, and re-layouts: 21.9 us -> 6.86 us
  between operations: 14.1 us -> 0.65 us
  starting transfers between devices: 4.53 us -> 0 us
  other arithmetic: 2.31 us -> 0 us
    pallas_call x0 -> x1, Pallas kernels: none -> 50.3 us  [on_device(): pl.pallas_call(functools.partial(fused_kernel, nf), out_shape=(jax.ShapeD...]
    unnamed x2 -> x0, waiting for transfers between devices: 41.1 us -> none
    all_to_all x1 -> x0, blocking collectives: 22 us -> none  [on_device(): lax.all_to_all(outgoing, 'expert', split_axis=0, concat_axis=0, tiled=True)]
    dot_general x6 -> x0, matrix products: 15.8 us -> none  [the longest x1 4.49 us: on_device(): jnp.einsum('sh,sd->hd', rows_in, grad_rows, preferred_element_type=jnp.fl...]
    all_to_all x1 -> x0, waiting for transfers between devices: 12.7 us -> none  [on_device(): lax.all_to_all(expert_out, 'expert', split_axis=0, concat_axis=0, tiled=T...]
    unnamed x15 -> x8, local copies, waits for them, and re-layouts: 14.4 us -> 6.86 us
    mul x3 -> x0, local copies, waits for them, and re-layouts: 7.24 us -> none  [the longest x2 7.11 us: on_device(): gate_grad = jnp.sum(gathered * grads_f[:, None, :], axis=2)]
    all_to_all x1 -> x0, starting transfers between devices: 4.49 us -> none  [on_device(): lax.all_to_all(expert_out, 'expert', split_axis=0, concat_axis=0, tiled=T...]
  transfers between devices with their start and end apart: 2 -> 0, of which waited for: 2 -> 0; matrix products, arithmetic and copies ran while one was open for 8% -> 0% of each run, Pallas kernels for 0% -> 0%
where the time goes in v1:
time: 58 us; the launch traced here: 57.8 us
  Pallas kernels  50.3 us (87%)
  local copies, waits for them, and re-layouts  6.86 us (12%)
  between operations  0.65 us (1%)
    pallas_call x1, Pallas kernels, on_device(): pl.pallas_call(functools.partial(fused_kernel, nf), out_shape=(jax.ShapeD...  50.3 us
    unnamed x8, local copies, waits for them, and re-layouts  6.86 us

profile of v1, /device:TPU:0, one launch (start us, length us, event | category | flops | bytes accessed | tf_op | source)
XLA Modules:
  0.0 57.8 jit_solution(4830727995351354131)
XLA Ops:
  0.6 0.8 %copy.9.ids_ref = s32[128,2]{1,0:T(8,128)S(1)} copy(s32[128,2]{0,1:T(2,128)} %param.5) | data formatting | bytes 2048 | tf_op args[0]
  1.4 0.8 %copy.10.gates_ref = f32[128,2]{1,0:T(8,128)S(1)} copy(f32[128,2]{0,1:T(2,128)} %param.6) | data formatting | bytes 2048 | tf_op args[1]
  2.2 0.0 copy-start
  2.2 1.0 %copy-done = bf16[1,1,4,80,768]{4,3,2,1,0:T(8,128)(2,1)S(1)} copy-done((bf16[1,1,4,80,768]{4,3,2,1,0:T(8,128)(2,1)S(1)}, bf16[1,1,4,80,768]{4,3,2,1,0:T(8,128)(2,1)}, u32[]{:S(2)}) %copy-start) | copy-done | bytes 491544
  3.2 50.3 %shard_map.84 = (bf16[128,2048]{1,0:T(8,128)(2,1)S(1)}, f32[128,2]{1,0:T(8,128)S(1)}, bf16[320,768]{1,0:T(8,128)(2,1)S(1)}, f32[96,2048]{1,0:T(8,128)}) custom-call(s32[128,2]{1,0:T(8,128)S(1)} %copy.9.ids_ref, f32[128,2]{1,0:T(8,128)S(1)} %copy.10.gates_ref, bf16[128,2048]{1,0:T(8,128)(2,1)} %og_ref.1, bf16[768,2048]{1,0:T(8,128)(2,1)} %bitcast.7, ...), custom_call_target="tpu_custom_call" | custom-call | flops 3019898880 | bytes 3145728 | tf_op jit(solution)/shard_map/pallas_call | solution.py:314
  53.5 0.6 %copy.11 = f32[128,2]{0,1:T(2,128)} copy(f32[128,2]{1,0:T(8,128)S(1)} %get-tuple-element.13) | data formatting | bytes 2048
  54.1 0.8 %copy.15 = bf16[128,2048]{1,0:T(8,128)(2,1)} copy(bf16[128,2048]{1,0:T(8,128)(2,1)S(1)} %get-tuple-element.20) | data formatting | bytes 1048576
  54.9 0.8 %copy.16 = bf16[1,1,4,80,768]{4,3,2,1,0:T(8,128)(2,1)} copy(bf16[1,1,4,80,768]{4,3,2,1,0:T(8,128)(2,1)S(1)} %bitcast.4) | data formatting | bytes 983040
  55.7 2.1 %copy.17 = f32[1,96,2048]{2,1,0:T(8,128)} copy(f32[1,96,2048]{2,1,0:T(8,128)} %bitcast.6) | data formatting | bytes 1572864
Async XLA Ops:
  2.2 1.0 %copy-start = (bf16[1,1,4,80,768]{4,3,2,1,0:T(8,128)(2,1)S(1)}, bf16[1,1,4,80,768]{4,3,2,1,0:T(8,128)(2,1)}, u32[]{:S(2)}) copy-start(bf16[1,1,4,80,768]{4,3,2,1,0:T(8,128)(2,1)} %param.9) | copy-start | bytes 1474564

commit v2 on v1

--- a/solution.py
+++ b/solution.py
@@ -10,6 +10,7 @@
 
 MESH = pl.DeviceIdType.MESH
 CHUNKS = 8
+AHEAD = 2
 F32 = jnp.float32
 BF16 = jnp.bfloat16
 
@@ -71,23 +72,29 @@
 
 
 def fused_kernel(
-    nf, ids_ref, gates_ref, og_ref, w_ref, hid_ref,
+    nf, ids_ref, gates_ref, og_hbm, w_hbm, hid_hbm,
     mixed_ref, gate_ref, hg_ref, wg_ref,
-    hall, ht, sel, sel_t, gslot, gcol, outg, inc, eo, ret, csend, crecv, acc,
+    og, wt, hid, hall, ht, sel, sel_t, gslot, gcol, outg, inc, eo, ret, csend, crecv, acc,
     rsend, rrecv, lsend, lrecv, hgacc, qacc,
-    cot_s, cot_r, eo_s, eo_r, core_s, core_r, rs, rr, ls, lr,
+    cot_s, cot_r, eo_s, eo_r, core_s, core_r, rs, rr, ls, lr, load,
 ):
     dp, me = lax.axis_index("dp"), lax.axis_index("expert")
     ne = lax.axis_size("expert")
     nz = lax.axis_size("dp") // 2
     z, core = lax.div(dp, 2), lax.rem(dp, 2)
-    tok, top = ids_ref.shape
+    top, tok = ids_ref.shape
     cap = inc.shape[2]
     fc = inc.shape[3]
-    width = hid_ref.shape[1]
     block = wg_ref.shape[0]
     slots = ne * cap
     mate = 2 * z + 1 - core
+
+    loads = [
+        pltpu.make_async_copy(src, dst, load.at[i])
+        for i, (src, dst) in enumerate(((og_hbm, og), (hid_hbm, hid), (w_hbm, wt)))
+    ]
+    for copy in loads:
+        copy.start()
 
     barrier = pltpu.get_barrier_semaphore()
     for d in range(1, ne):
@@ -107,23 +114,26 @@
     row = lax.broadcasted_iota(jnp.int32, (tok, tok), 0)
     col = lax.broadcasted_iota(jnp.int32, (tok, tok), 1)
     diagonal = row == col
-    earlier = col < row
+    earlier = row < col
     slot_rows = lax.broadcasted_iota(jnp.int32, (cap, tok), 0).astype(F32)
     slot_cols = lax.broadcasted_iota(jnp.int32, (tok, cap), 1).astype(F32)
 
-    def to_row(column):
-        return jnp.sum(jnp.where(diagonal, column, 0.0), axis=0, keepdims=True)
+    def to_column(values):
+        return jnp.sum(jnp.where(diagonal, values, 0.0), axis=1, keepdims=True)
+
+    def to_row(values):
+        return jnp.sum(jnp.where(diagonal, values, 0.0), axis=0, keepdims=True)
 
     for e in range(ne):
-        named = jnp.sum(jnp.where(ids == e, 1.0, 0.0), axis=1, keepdims=True)
-        gate = jnp.sum(jnp.where(ids == e, gates, 0.0), axis=1, keepdims=True)
-        rank = jnp.sum(jnp.where(earlier, to_row(named), 0.0), axis=1, keepdims=True)
+        named = jnp.sum(jnp.where(ids == e, 1.0, 0.0), axis=0, keepdims=True)
+        gate = jnp.sum(jnp.where(ids == e, gates, 0.0), axis=0, keepdims=True)
+        rank = jnp.sum(jnp.where(earlier, to_column(named), 0.0), axis=0, keepdims=True)
         place = jnp.where(named > 0.0, rank, -1.0)
-        hit = slot_rows == to_row(place)
+        hit = slot_rows == place
         sel[e] = jnp.where(hit, 1.0, 0.0).astype(BF16)
-        gslot[e] = jnp.sum(jnp.where(hit, to_row(gate), 0.0), axis=1, keepdims=True)
-        sel_t[e] = jnp.where(slot_cols == place, 1.0, 0.0).astype(BF16)
-        gcol[e] = gate
+        gslot[e] = jnp.sum(jnp.where(hit, gate, 0.0), axis=1, keepdims=True)
+        sel_t[e] = jnp.where(slot_cols == to_column(place), 1.0, 0.0).astype(BF16)
+        gcol[e] = to_column(gate)
 
     count = ne + jnp.where(z > 0, 1, 0) + jnp.where(z < nz - 1, 1, 0)
     pl.semaphore_wait(barrier, count)
@@ -149,21 +159,20 @@
             send_sem=core_s.at[f], recv_sem=core_r.at[f],
             device_id=(mate, me), device_id_type=MESH)
 
-    def up_copy(f, zz):
+    def up_copy(f, k):
         return pltpu.make_async_remote_copy(
-            src_ref=rsend.at[f, zz], dst_ref=rrecv.at[f, zz],
-            send_sem=rs.at[f, zz], recv_sem=rr.at[f, zz],
+            src_ref=rsend.at[f, k], dst_ref=rrecv.at[f, k],
+            send_sem=rs.at[f, k], recv_sem=rr.at[f, k],
             device_id=(lax.rem(dp + 2, 2 * nz), me), device_id_type=MESH)
 
-    def down_copy(f, zz):
+    def down_copy(f, k):
         return pltpu.make_async_remote_copy(
-            src_ref=lsend.at[f, zz], dst_ref=lrecv.at[f, zz],
-            send_sem=ls.at[f, zz], recv_sem=lr.at[f, zz],
+            src_ref=lsend.at[f, k], dst_ref=lrecv.at[f, k],
+            send_sem=ls.at[f, k], recv_sem=lr.at[f, k],
             device_id=(lax.rem(dp + 2 * nz - 2, 2 * nz), me), device_id_type=MESH)
 
-    @pl.loop(0, nf)
-    def _(f):
-        grads = og_ref[:, columns(f)]
+    def send_cotangents(f):
+        grads = og[:, columns(f)]
         for d in (*range(1, ne), 0):
             e = lax.rem(me + d, ne)
             rows = jnp.dot(sel[e], grads, preferred_element_type=F32)
@@ -174,10 +183,18 @@
             else:
                 inc[f, me] = rows
 
-    hall[...] = hid_ref[...].T
+    loads[0].wait()
+
+    @pl.loop(0, AHEAD)
+    def _(f):
+        send_cotangents(f)
+
+    loads[1].wait()
+    hall[...] = hid[...].T
     for zz in range(nz):
         ht[0, zz] = hall[pl.ds(pl.multiple_of(block * (2 * zz + 1 - core), block), block), :]
         ht[1, zz] = hall[pl.ds(pl.multiple_of(block * (2 * zz + core), block), block), :]
+    loads[2].wait()
     hgacc[...] = jnp.zeros_like(hgacc)
     qacc[...] = jnp.zeros_like(qacc)
 
@@ -186,9 +203,11 @@
         @pl.when(s < nf)
         def _():
             f = s
-            weight = w_ref[:, columns(f)]
-            y = jnp.dot(hid_ref[...], weight, preferred_element_type=F32)
-            eo[f] = y.astype(BF16).reshape(ne, cap, fc)
+
+            @pl.when(f + AHEAD < nf)
+            def _():
+                send_cotangents(f + AHEAD)
+
             for d in range(1, ne):
                 e = lax.rem(me + ne - d, ne)
                 cot_copy(f, d, e, e).wait_recv()
@@ -196,48 +215,48 @@
             other = jnp.dot(ht[0].reshape(nz * block, slots), x, preferred_element_type=F32)
             csend[f] = other.astype(BF16).reshape(nz, block, fc)
             core_copy(f).start()
+            own = jnp.dot(ht[1].reshape(nz * block, slots), x, preferred_element_type=F32)
+            acc[f] = own.reshape(nz, block, fc)
+            weight = wt[:, columns(f)]
+            y = jnp.dot(hid[...], weight, preferred_element_type=F32)
+            eo[f] = y.astype(BF16).reshape(ne, cap, fc)
             for d in range(1, ne):
                 e = lax.rem(me + d, ne)
                 eo_copy(f, d, e, me).start()
             ret[f, me] = eo[f, me]
-            own = jnp.dot(ht[1].reshape(nz * block, slots), x, preferred_element_type=F32)
-            acc[f] = own.reshape(nz, block, fc)
-            hgacc[...] += lax.dot_general(
-                x, weight, (((1,), (1,)), ((), ())), preferred_element_type=F32)
             core_copy(f).wait_recv()
             acc[f] += crecv[f].astype(F32)
 
-        up = s - z
-
-        @pl.when((up >= 0) & (up < nf))
+        for k in range(nz):
+            up = s - k
+
+            @pl.when((z == k) & (up >= 0) & (up < nf))
+            def _():
+                for zz in range(nz - 1, k, -1):
+                    term = acc[up, zz]
+                    if k > 0:
+                        up_copy(up, zz).wait_recv()
+                        term += rrecv[up, zz].astype(F32)
+                    rsend[up, zz] = term.astype(BF16)
+                    up_copy(up, zz).start()
+
+            down = s - (nz - 1 - k)
+
+            @pl.when((z == k) & (down >= 0) & (down < nf))
+            def _():
+                for zz in range(k):
+                    term = acc[down, zz]
+                    if k < nz - 1:
+                        down_copy(down, zz).wait_recv()
+                        term += lrecv[down, zz].astype(F32)
+                    lsend[down, zz] = term.astype(BF16)
+                    down_copy(down, zz).start()
+
+        @pl.when(s < nf)
         def _():
-            for zz in range(nz - 1, 0, -1):
-                @pl.when((zz > z) & (z > 0))
-                def _():
-                    up_copy(up, zz).wait_recv()
-                    rsend[up, zz] = (acc[up, zz] + rrecv[up, zz].astype(F32)).astype(BF16)
-                    up_copy(up, zz).start()
-
-                @pl.when((zz > z) & (z == 0))
-                def _():
-                    rsend[up, zz] = acc[up, zz].astype(BF16)
-                    up_copy(up, zz).start()
-
-        down = s - (nz - 1 - z)
-
-        @pl.when((down >= 0) & (down < nf))
-        def _():
-            for zz in range(nz - 1):
-                @pl.when((zz < z) & (z < nz - 1))
-                def _():
-                    down_copy(down, zz).wait_recv()
-                    lsend[down, zz] = (acc[down, zz] + lrecv[down, zz].astype(F32)).astype(BF16)
-                    down_copy(down, zz).start()
-
-                @pl.when((zz < z) & (z == nz - 1))
-                def _():
-                    lsend[down, zz] = acc[down, zz].astype(BF16)
-                    down_copy(down, zz).start()
+            hgacc[...] += lax.dot_general(
+                inc[s].reshape(slots, fc), wt[:, columns(s)],
+                (((1,), (1,)), ((), ())), preferred_element_type=F32)
 
         back = s - (nz - 1)
 
@@ -247,7 +266,7 @@
             for d in range(1, ne):
                 e = lax.rem(me + ne - d, ne)
                 eo_copy(f, d, e, e).wait_recv()
-            grads = og_ref[:, columns(f)].astype(F32)
+            grads = og[:, columns(f)].astype(F32)
             mixed = jnp.zeros((tok, fc), F32)
             for e in range(ne):
                 routed = jnp.dot(sel_t[e], ret[f, e], preferred_element_type=F32)
@@ -272,14 +291,12 @@
                 wg_ref[:, columns(f)] += lrecv[f, z].astype(F32)
 
     hg_ref[...] = hgacc[...].astype(BF16)
-    parts = []
+    sums = [to_row(jnp.sum(qacc[e], axis=1, keepdims=True)) for e in range(ne)]
     for k in range(top):
-        total = jnp.zeros((tok, 1), F32)
+        total = jnp.zeros((1, tok), F32)
         for e in range(ne):
-            total += jnp.where(ids[:, k:k + 1] == e, jnp.sum(qacc[e], axis=1, keepdims=True), 0.0)
-        parts.append(total)
-    for k in range(top):
-        gate_ref[:, k:k + 1] = parts[k]
+            total += jnp.where(ids[k:k + 1, :] == e, sums[e], 0.0)
+        gate_ref[k:k + 1, :] = total
 
     @pl.loop(0, nf)
     def _(f):
@@ -288,14 +305,13 @@
             e = lax.rem(me + d, ne)
             cot_copy(f, d, e, me).wait_send()
             eo_copy(f, d, e, me).wait_send()
-        for zz in range(nz):
-            @pl.when(zz > z)
-            def _():
-                up_copy(f, zz).wait_send()
-
-            @pl.when(zz < z)
-            def _():
-                down_copy(f, zz).wait_send()
+        for k in range(nz):
+            @pl.when(z == k)
+            def _():
+                for zz in range(k + 1, nz):
+                    up_copy(f, zz).wait_send()
+                for zz in range(k):
+                    down_copy(f, zz).wait_send()
 
 
 def on_device(route_ids, gate_values, out_grad, down_weight, hidden):
@@ -311,17 +327,22 @@
     chain = pltpu.VMEM((nf, nz, block, fc), BF16)
     dma = pltpu.SemaphoreType.DMA
     vmem = pl.BlockSpec(memory_space=pltpu.VMEM)
+    out_shape = (
+        jax.ShapeDtypeStruct((tok, feat), BF16),
+        jax.ShapeDtypeStruct((top, tok), F32),
+        jax.ShapeDtypeStruct((slots, width), BF16),
+        jax.ShapeDtypeStruct((block, feat), F32),
+    )
+    hbm = pl.BlockSpec(memory_space=pltpu.HBM)
     mixed, gate, hg, wg = pl.pallas_call(
         functools.partial(fused_kernel, nf),
-        out_shape=(
-            jax.ShapeDtypeStruct((tok, feat), BF16),
-            jax.ShapeDtypeStruct((tok, top), F32),
-            jax.ShapeDtypeStruct((slots, width), BF16),
-            jax.ShapeDtypeStruct((block, feat), F32),
-        ),
-        in_specs=[vmem] * 5,
+        out_shape=out_shape,
+        in_specs=[vmem, vmem, hbm, hbm, hbm],
         out_specs=(vmem,) * 4,
         scratch_shapes=[
+            pltpu.VMEM((tok, feat), BF16),
+            pltpu.VMEM((width, feat), BF16),
+            pltpu.VMEM((slots, width), BF16),
             pltpu.VMEM((width, slots), BF16),
             pltpu.VMEM((2, nz, block, slots), BF16),
             pltpu.VMEM((ne, cap, tok), BF16),
@@ -351,6 +372,7 @@
             dma((nf, nz)),
             dma((nf, nz)),
             dma((nf, nz)),
+            dma((3,)),
         ],
         compiler_params=pltpu.CompilerParams(
             collective_id=0, has_side_effects=True, vmem_limit_bytes=52 * 1024 * 1024
@@ -358,8 +380,8 @@
         cost_estimate=pl.CostEstimate(
             flops=6 * slots * width * feat, bytes_accessed=2 * width * feat, transcendentals=0
         ),
-    )(route_ids, gate_values, out_grad, down_weight[0], hidden.reshape(slots, width))
-    return mixed, gate, hg.reshape(hidden.shape), wg[None]
+    )(route_ids.T, gate_values.T, out_grad, down_weight[0], hidden.reshape(slots, width))
+    return mixed, gate.T, hg.reshape(hidden.shape), wg[None]
 
 
 def fits(mesh):

time: 58 us -> 54.2 us (0.934)
  Pallas kernels: 50.3 us -> 46.8 us
    pallas_call x1, Pallas kernels: 50.3 us -> 46.8 us  [on_device(): pl.pallas_call(functools.partial(fused_kernel, nf), out_shape=out_shape,...]
    unnamed x8 -> x10, local copies, waits for them, and re-layouts: 6.86 us -> 6.58 us
where the time goes in v2:
time: 54.2 us; the launch traced here: 54 us
  Pallas kernels  46.8 us (86%)
  local copies, waits for them, and re-layouts  6.58 us (12%)
  between operations  0.65 us (1%)
    pallas_call x1, Pallas kernels, on_device(): pl.pallas_call(functools.partial(fused_kernel, nf), out_shape=out_shape,...  46.8 us
    unnamed x10, local copies, waits for them, and re-layouts  6.58 us

profile of v2, /device:TPU:0, one launch (start us, length us, event | category | flops | bytes accessed | tf_op | source)
XLA Modules:
  0.0 54.0 jit_solution(16654364953771255996)
XLA Ops:
  0.6 0.0 copy-start
  0.6 1.0 %copy-done = bf16[1,1,4,80,768]{4,3,2,1,0:T(8,128)(2,1)S(1)} copy-done((bf16[1,1,4,80,768]{4,3,2,1,0:T(8,128)(2,1)S(1)}, bf16[1,1,4,80,768]{4,3,2,1,0:T(8,128)(2,1)}, u32[]{:S(2)}) %copy-start) | copy-done | bytes 491544
  1.7 0.0 copy-start.1
  1.7 0.7 %copy-done.1 = s32[128,2]{0,1:T(2,128)S(1)} copy-done((s32[128,2]{0,1:T(2,128)S(1)}, s32[128,2]{0,1:T(2,128)}, u32[]{:S(2)}) %copy-start.1) | copy-done | bytes 1048
  2.3 0.0 copy-start.2
  2.3 0.7 %copy-done.2 = f32[128,2]{0,1:T(2,128)S(1)} copy-done((f32[128,2]{0,1:T(2,128)S(1)}, f32[128,2]{0,1:T(2,128)}, u32[]{:S(2)}) %copy-start.2) | copy-done | bytes 1048
  3.0 46.8 %shard_map.84 = (bf16[128,2048]{1,0:T(8,128)(2,1)S(1)}, f32[2,128]{1,0:T(2,128)S(1)}, bf16[320,768]{1,0:T(8,128)(2,1)S(1)}, f32[96,2048]{1,0:T(8,128)}) custom-call(s32[2,128]{1,0:T(2,128)S(1)} %bitcast.10, f32[2,128]{1,0:T(2,128)S(1)} %bitcast.11, bf16[128,2048]{1,0:T(8,128)(2,1)} %og_hbm.1, bf16[768,2048]{1,0:T(8,128)(2,1)} %bitcast.13, ...), custom_call_target="tpu_custom_call" | custom-call | flops 3019898880 | bytes 3145728 | tf_op jit(solution)/shard_map/pallas_call | solution.py:337
  49.8 0.8 %copy.13 = bf16[128,2048]{1,0:T(8,128)(2,1)} copy(bf16[128,2048]{1,0:T(8,128)(2,1)S(1)} %get-tuple-element.16) | data formatting | bytes 1048576
  50.6 0.6 %copy.14 = f32[128,2]{0,1:T(2,128)} copy(f32[128,2]{0,1:T(2,128)S(1)} %bitcast.8) | data formatting | bytes 2048
  51.2 0.8 %copy.15 = bf16[1,1,4,80,768]{4,3,2,1,0:T(8,128)(2,1)} copy(bf16[1,1,4,80,768]{4,3,2,1,0:T(8,128)(2,1)S(1)} %bitcast.7) | data formatting | bytes 983040
  51.9 2.1 %copy.16 = f32[1,96,2048]{2,1,0:T(8,128)} copy(f32[1,96,2048]{2,1,0:T(8,128)} %bitcast.12) | data formatting | bytes 1572864
Async XLA Ops:
  0.6 1.0 %copy-start = (bf16[1,1,4,80,768]{4,3,2,1,0:T(8,128)(2,1)S(1)}, bf16[1,1,4,80,768]{4,3,2,1,0:T(8,128)(2,1)}, u32[]{:S(2)}) copy-start(bf16[1,1,4,80,768]{4,3,2,1,0:T(8,128)(2,1)} %param.9) | copy-start | bytes 1474564
  1.7 0.7 %copy-start.1 = (s32[128,2]{0,1:T(2,128)S(1)}, s32[128,2]{0,1:T(2,128)}, u32[]{:S(2)}) copy-start(s32[128,2]{0,1:T(2,128)} %param.5) | copy-start | bytes 3076
  2.3 0.7 %copy-start.2 = (f32[128,2]{0,1:T(2,128)S(1)}, f32[128,2]{0,1:T(2,128)}, u32[]{:S(2)}) copy-start(f32[128,2]{0,1:T(2,128)} %param.6) | copy-start | bytes 3076

commit v3 on v2

--- a/solution.py
+++ b/solution.py
@@ -224,6 +224,8 @@
                 e = lax.rem(me + d, ne)
                 eo_copy(f, d, e, me).start()
             ret[f, me] = eo[f, me]
+            hgacc[...] += lax.dot_general(
+                x, weight, (((1,), (1,)), ((), ())), preferred_element_type=F32)
             core_copy(f).wait_recv()
             acc[f] += crecv[f].astype(F32)
 
@@ -251,12 +253,6 @@
                         term += lrecv[down, zz].astype(F32)
                     lsend[down, zz] = term.astype(BF16)
                     down_copy(down, zz).start()
-
-        @pl.when(s < nf)
-        def _():
-            hgacc[...] += lax.dot_general(
-                inc[s].reshape(slots, fc), wt[:, columns(s)],
-                (((1,), (1,)), ((), ())), preferred_element_type=F32)
 
         back = s - (nz - 1)
 

time: 54.2 us -> 54.1 us (level)
  no operation moved by 1% of the time
where the time goes in v3:
time: 54.1 us; the launch traced here: 53.8 us
  Pallas kernels  46.6 us (86%)
  local copies, waits for them, and re-layouts  6.58 us (12%)
  between operations  0.65 us (1%)
    pallas_call x1, Pallas kernels, on_device(): pl.pallas_call(functools.partial(fused_kernel, nf), out_shape=out_shape,...  46.6 us
    unnamed x10, local copies, waits for them, and re-layouts  6.58 us

profile of v3, /device:TPU:0, one launch (start us, length us, event | category | flops | bytes accessed | tf_op | source)
XLA Modules:
  0.0 53.8 jit_solution(8884675339157334927)
XLA Ops:
  0.6 0.0 copy-start
  0.6 1.0 %copy-done = bf16[1,1,4,80,768]{4,3,2,1,0:T(8,128)(2,1)S(1)} copy-done((bf16[1,1,4,80,768]{4,3,2,1,0:T(8,128)(2,1)S(1)}, bf16[1,1,4,80,768]{4,3,2,1,0:T(8,128)(2,1)}, u32[]{:S(2)}) %copy-start) | copy-done | bytes 491544
  1.7 0.0 copy-start.1
  1.7 0.7 %copy-done.1 = s32[128,2]{0,1:T(2,128)S(1)} copy-done((s32[128,2]{0,1:T(2,128)S(1)}, s32[128,2]{0,1:T(2,128)}, u32[]{:S(2)}) %copy-start.1) | copy-done | bytes 1048
  2.3 0.0 copy-start.2
  2.3 0.7 %copy-done.2 = f32[128,2]{0,1:T(2,128)S(1)} copy-done((f32[128,2]{0,1:T(2,128)S(1)}, f32[128,2]{0,1:T(2,128)}, u32[]{:S(2)}) %copy-start.2) | copy-done | bytes 1048
  3.0 46.6 %shard_map.84 = (bf16[128,2048]{1,0:T(8,128)(2,1)S(1)}, f32[2,128]{1,0:T(2,128)S(1)}, bf16[320,768]{1,0:T(8,128)(2,1)S(1)}, f32[96,2048]{1,0:T(8,128)}) custom-call(s32[2,128]{1,0:T(2,128)S(1)} %bitcast.10, f32[2,128]{1,0:T(2,128)S(1)} %bitcast.11, bf16[128,2048]{1,0:T(8,128)(2,1)} %og_hbm.1, bf16[768,2048]{1,0:T(8,128)(2,1)} %bitcast.13, ...), custom_call_target="tpu_custom_call" | custom-call | flops 3019898880 | bytes 3145728 | tf_op jit(solution)/shard_map/pallas_call | solution.py:333
  49.6 0.8 %copy.13 = bf16[128,2048]{1,0:T(8,128)(2,1)} copy(bf16[128,2048]{1,0:T(8,128)(2,1)S(1)} %get-tuple-element.16) | data formatting | bytes 1048576
  50.4 0.6 %copy.14 = f32[128,2]{0,1:T(2,128)} copy(f32[128,2]{0,1:T(2,128)S(1)} %bitcast.8) | data formatting | bytes 2048
  51.0 0.8 %copy.15 = bf16[1,1,4,80,768]{4,3,2,1,0:T(8,128)(2,1)} copy(bf16[1,1,4,80,768]{4,3,2,1,0:T(8,128)(2,1)S(1)} %bitcast.7) | data formatting | bytes 983040
  51.8 2.1 %copy.16 = f32[1,96,2048]{2,1,0:T(8,128)} copy(f32[1,96,2048]{2,1,0:T(8,128)} %bitcast.12) | data formatting | bytes 1572864
Async XLA Ops:
  0.6 1.0 %copy-start = (bf16[1,1,4,80,768]{4,3,2,1,0:T(8,128)(2,1)S(1)}, bf16[1,1,4,80,768]{4,3,2,1,0:T(8,128)(2,1)}, u32[]{:S(2)}) copy-start(bf16[1,1,4,80,768]{4,3,2,1,0:T(8,128)(2,1)} %param.9) | copy-start | bytes 1474564
  1.7 0.7 %copy-start.1 = (s32[128,2]{0,1:T(2,128)S(1)}, s32[128,2]{0,1:T(2,128)}, u32[]{:S(2)}) copy-start(s32[128,2]{0,1:T(2,128)} %param.5) | copy-start | bytes 3076
  2.3 0.7 %copy-start.2 = (f32[128,2]{0,1:T(2,128)S(1)}, f32[128,2]{0,1:T(2,128)}, u32[]{:S(2)}) copy-start(f32[128,2]{0,1:T(2,128)} %param.6) | copy-start | bytes 3076
